TPU v7x, 32 devices: a whole 2x2x4 slice. The times are simulated.
32 devices in a mesh: grp: 2 (over x), row: 8 (over z, y), col: 2 (over core).
Axes of the slice: x: 2, y: 2, z: 4, core: 2. Of those that a mesh axis runs over, the one named last changes fastest.
Arguments:
- pair: bfloat16 [128, 64, 128], P(('grp', 'row'), 'col'), parts along dimension 0, may hold values from -6 to 6
- pair_mask: int32 [128, 64], P(('grp', 'row'), 'col'), parts along dimension 0, may hold values 0 or 1
- chain_ids: int32 [128], P('grp'), parts along dimension 0, may hold values from 0 to 3, never falling along the last dimension, each value on 1 to 32 neighbouring positions
- norm_gain: float32 [128], replicated, may hold values from 0.1 to 1.9
- norm_shift: float32 [128], replicated, may hold values from -3 to 3
- w_proj: bfloat16 [128, 512], replicated, may hold values from -0.5 to 0.5
- w_gate: bfloat16 [128, 128], replicated, may hold values from -0.5 to 0.5
- gate_bias: float32 [2, 128], replicated, may hold values from -4 to 4
- out_gain: float32 [128], replicated, may hold values from 0.1 to 1.9
- out_shift: float32 [128], replicated, may hold values from -3 to 3
- w_out: bfloat16 [128, 128], replicated, may hold values from -0.5 to 0.5
Outputs:
- update: bfloat16 [128, 64, 128], P(('grp', 'row'), 'col'), parts along dimension 0
There are 2 independent parts, one for each index of `grp`. A program takes and returns all parts, laid end to end along the dimension named above; an argument that names none is the same for every part. Nothing has to cross between parts.
Inputs may be any that keep to these rules, and one draw needn't show every extreme that they name: `chain_ids`: chain ids never fall along the residues; each chain holds 1 to 32 residues, one exactly 32.
All inputs are finite; a program needn't handle non-finite values. No bound on the sum of `pair_mask` on one device may be relied on, other than what follows from the above.
Results may differ from a plain program's by a relative error of at most 0.0062.
Values may be sent and summed in bfloat16 or wider, within the bound.
A program may use at most 192 MiB of HBM per device.

v0:
```python
import jax
import jax.numpy as jnp
from jax import lax
from jax.sharding import PartitionSpec as P


def layer_norm(values, gain, shift):
    mean = jnp.mean(values, axis=-1, keepdims=True)
    centred = values - mean
    variance = jnp.mean(centred * centred, axis=-1, keepdims=True)
    return centred * lax.rsqrt(variance + 1e-05) * gain + shift


def shards(
    pair,
    pair_mask,
    chain_ids,
    norm_gain,
    norm_shift,
    w_proj,
    w_gate,
    gate_bias,
    out_gain,
    out_shift,
    w_out,
):
    tile_rows = pair.shape[0]
    tile_cols = pair.shape[1]
    channels = pair.shape[2]
    hidden_width = w_out.shape[0]
    normed = layer_norm(pair.astype(jnp.float32), norm_gain, norm_shift).astype(jnp.bfloat16)
    flat = normed.reshape(tile_rows * tile_cols, channels)
    proj = jnp.dot(flat, w_proj, preferred_element_type=jnp.float32).reshape(
        tile_rows, tile_cols, 4, hidden_width
    )
    mask_float = pair_mask.astype(jnp.float32)[:, :, None]
    left_side = (mask_float * jax.nn.sigmoid(proj[:, :, 1]) * proj[:, :, 0]).astype(jnp.bfloat16)
    right_side = (mask_float * jax.nn.sigmoid(proj[:, :, 3]) * proj[:, :, 2]).astype(jnp.bfloat16)
    partial_sums = jnp.einsum(
        "ikc,jkc->ijc",
        left_side,
        lax.all_gather(right_side, "row", axis=0, tiled=True),
        preferred_element_type=jnp.float32,
    )
    combined = lax.psum_scatter(partial_sums, "col", scatter_dimension=1, tiled=True)
    hidden = layer_norm(combined, out_gain, out_shift).astype(jnp.bfloat16)
    projected = jnp.dot(
        hidden.reshape(tile_rows * tile_cols, hidden_width),
        w_out,
        preferred_element_type=jnp.float32,
    )
    projected = projected.reshape(tile_rows, tile_cols, channels)
    row_start = lax.axis_index("row") * tile_rows
    col_start = lax.axis_index("col") * tile_cols
    row_chain = lax.dynamic_slice_in_dim(chain_ids, row_start, tile_rows)
    col_chain = lax.dynamic_slice_in_dim(chain_ids, col_start, tile_cols)
    same_chain = (row_chain[:, None] == col_chain[None, :])[:, :, None]
    gate_logit = jnp.dot(flat, w_gate, preferred_element_type=jnp.float32).reshape(
        tile_rows, tile_cols, channels
    )
    gate_logit = gate_logit + jnp.where(same_chain, gate_bias[0], gate_bias[1])
    return (jax.nn.sigmoid(gate_logit) * projected).astype(jnp.bfloat16)


def solution(mesh):
    return jax.shard_map(
        shards,
        mesh=mesh,
        in_specs=(
            P(("grp", "row"), "col", None),
            P(("grp", "row"), "col"),
            P("grp"),
            P(),
            P(),
            P(),
            P(),
            P(),
            P(),
            P(),
            P(),
        ),
        out_specs=P(("grp", "row"), "col", None),
        check_vma=False,
    )
```

profile of v0, /device:TPU:1, one launch (start us, length us, event | category | flops | bytes accessed | tf_op | source)
XLA Modules:
  0.0 69.7 jit_solution(10805145590867093489)
XLA Ops:
  6.5 0.9 %convert_reduce_fusion = f32[8,32]{1,0:T(8,128)S(1)} fusion(bf16[8,32,128]{2,1,0:T(8,128)(2,1)} %param.11), kind=kLoop, calls=%fused_computation.9 | loop fusion | flops 65280 | bytes 66560 | tf_op jit(solution)/shard_map/reduce_sum | solution.py:8
  7.5 1.0 %fusion.7 = f32[8,32]{1,0:T(8,128)S(1)} fusion(bf16[8,32,128]{2,1,0:T(8,128)(2,1)} %param.11, f32[8,32]{1,0:T(8,128)S(1)} %broadcast_multiply_fusion.1), kind=kLoop, calls=%fused_computation.12 | loop fusion | flops 130816 | bytes 67584 | tf_op jit(solution)/shard_map/reduce_sum | solution.py:10
  8.5 1.0 %copy.52 = bf16[512,128]{1,0:T(8,128)(2,1)S(1)} copy(bf16[512,128]{0,1:T(8,128)(2,1)} %bitcast.83) | data formatting | bytes 262144 | tf_op jit(solution)/shard_map/dot_general | solution.py:33
  9.6 0.7 convert_element_type.23
  10.3 1.1 %fusion.27 = f32[8,32,4,128]{3,1,2,0:T(8,128)S(1)} fusion(bf16[4,128,128,1]{2,1,0,3:T(8,128)(2,1)S(1)} %bitcast.82, bf16[8,32,128]{2,1,0:T(8,128)(2,1)} %param.11, f32[128]{0:T(128)} %param.15, f32[128]{0:T(128)} %param.14, f32[8,32]{1,0:T(8,128)S(1)} %add_rsqrt_fusion.1, f32[8,32]{1,0:T(8,128)S(1)} %broadcast_multiply_fusion.1), kind=kOutput, calls=%fused_computation.38 | convolution fusion | flops 33751040 | bytes 723968 | tf_op jit(solution)/shard_map/dot_general | solution.py:33
  11.4 0.1 fusion.12
  11.5 26.9 %all_gather.3 = bf16[64,32,128]{2,1,0:T(8,128)(2,1)S(1)} all-gather(bf16[8,32,128]{2,1,0:T(8,128)(2,1)S(1)} %get-tuple-element.6), channel_id=1, replica_groups=mesh['grp'=2,'row'=8,'col'=2] {'row'}, dimensions={0}, use_global_device_ids=true | all-gather | bytes 589824 | tf_op jit(solution)/shard_map/all_gather | solution.py:42
  38.5 3.0 %copy.43 = bf16[64,32,128]{1,0,2:T(8,128)(2,1)S(1)} copy(bf16[64,32,128]{2,1,0:T(8,128)(2,1)S(1)} %all_gather.3) | data formatting | bytes 1048576 | tf_op jit(solution)/shard_map/all_gather | solution.py:42
  41.5 0.0 copy-start.3
  41.5 0.0 copy-start.8
  41.5 0.0 copy-start.1
  41.5 0.0 copy-start.6
  41.5 0.0 copy-start.7
  41.5 0.2 copy.44
  41.7 0.0 copy-start.4
  41.7 0.0 copy-start.2
  41.7 1.2 %convolution_bitcast_fusion = f32[8,64,128]{1,0,2:T(8,128)S(1)} fusion(bf16[64,32,128]{1,0,2:T(8,128)(2,1)S(1)} %copy.43, bf16[8,32,128]{1,0,2:T(8,128)(2,1)S(1)} %copy.44), kind=kOutput, calls=%fused_computation | convolution fusion | flops 4194304 | bytes 851968 | tf_op jit(solution)/shard_map/ikc,jkc->ijc/dot_general | solution.py:39
  42.9 0.9 %copy.45 = f32[8,64,128]{2,0,1:T(8,128)} copy(f32[8,64,128]{1,0,2:T(8,128)S(1)} %convolution_bitcast_fusion) | data formatting | bytes 524288 | tf_op jit(solution)/shard_map/ikc,jkc->ijc/transpose | solution.py:39
  43.8 0.0 reduce-scatter.2.cloned.1.call-update
  43.9 0.1 dynamic_slice.6
  44.0 0.1 dynamic_slice.7
  44.1 0.1 broadcast_compare_fusion
  44.2 0.3 fusion.3
  44.4 14.2 %reduce-scatter.2.cloned.1.call-done = f32[8,32,128]{2,0,1:T(8,128)} async-done(((f32[8,64,128]{2,0,1:T(8,128)}), f32[8,32,128]{2,0,1:T(8,128)}) %reduce-scatter.2.cloned.1.call-update) | async-done | bytes 131088 | tf_op jit(solution)/shard_map/reduce_scatter | solution.py:45
  58.6 1.0 %reduce_sum.38 = f32[8,32]{0,1:T(8,128)S(1)} reduce(f32[8,32,128]{2,0,1:T(8,128)} %reduce-scatter.2.cloned.1.call-done, f32[]{:T(128)} %constant.7.clone.1), dimensions={2}, to_apply=%region_3.0 | reduce | flops 32512 | bytes 132100 | tf_op jit(solution)/shard_map/reduce_sum | solution.py:8
  59.6 0.1 copy.46
  59.7 0.1 copy.47
  59.8 1.1 %multiply_reduce_fusion = f32[8,32]{0,1:T(8,128)S(1)} fusion(f32[8,32,128]{2,0,1:T(8,128)} %reduce-scatter.2.cloned.1.call-done, f32[8,32]{0,1:T(8,128)S(1)} %copy.47), kind=kLoop, calls=%fused_computation.37 | loop fusion | flops 98048 | bytes 133120 | tf_op jit(solution)/shard_map/reduce_sum | solution.py:10
  60.9 0.1 copy.48
  60.9 0.1 copy.49
  61.0 1.0 %add_convert_fusion = bf16[8,32,128]{2,0,1:T(8,128)(2,1)S(1)} fusion(f32[8,32,128]{2,0,1:T(8,128)} %reduce-scatter.2.cloned.1.call-done, f32[128]{0:T(128)S(1)} %copy-done.4, f32[128]{0:T(128)S(1)} %copy-done.5, f32[8,32]{0,1:T(8,128)S(1)} %copy.49, f32[8,32]{0,1:T(8,128)S(1)} %copy.47), kind=kLoop, calls=%fused_computation.36 | loop fusion | flops 163840 | bytes 199680 | tf_op jit(solution)/shard_map/convert_element_type | solution.py:46
  62.1 0.8 %fusion.4 = bf16[8,32,128]{2,1,0:T(8,128)(2,1)} fusion(f32[8,32,128]{2,1,0:T(8,128)S(1)} %fusion.3, bf16[8,32,128]{2,0,1:T(8,128)(2,1)S(1)} %add_convert_fusion, bf16[128,128]{1,0:T(8,128)(2,1)S(1)} %copy-done.2), kind=kOutput, calls=%fused_computation.7 | convolution fusion | flops 8454144 | bytes 294912 | tf_op jit(solution)/shard_map/dot_general | solution.py:47
  (17 shorter events, 0.1 us)
Async XLA Ops:
  6.5 37.6 %copy-start = (bf16[128,128]{1,0:T(8,128)(2,1)S(1)}, bf16[128,128]{1,0:T(8,128)(2,1)}, u32[]{:S(2)}) copy-start(bf16[128,128]{1,0:T(8,128)(2,1)} %param.17) | copy-start | bytes 98308
  6.5 52.1 %reduce-scatter.2.cloned.1.call-start = ((), (), s32[]{:S(2)}) async-start(), calls=%async_computation.1 | async-start | bytes 393216 | tf_op jit(solution)/shard_map/reduce_scatter | solution.py:45
  41.5 2.4 %copy-start.3 = (f32[2,128]{1,0:T(2,128)S(1)}, f32[2,128]{1,0:T(2,128)}, u32[]{:S(2)}) copy-start(f32[2,128]{1,0:T(2,128)} %param.18) | copy-start | bytes 3076
  41.5 2.4 %copy-start.8 = (s32[64]{0:T(128)S(1)}, s32[64]{0:T(128)}, u32[]{:S(2)}) copy-start(s32[64]{0:T(128)} %param.13) | copy-start | bytes 772
  41.5 2.7 %copy-start.1 = (bf16[8,32,128]{2,1,0:T(8,128)(2,1)S(1)}, bf16[8,32,128]{2,1,0:T(8,128)(2,1)}, u32[]{:S(2)}) copy-start(bf16[8,32,128]{2,1,0:T(8,128)(2,1)} %param.11) | copy-start | bytes 196612
  41.5 2.7 %copy-start.6 = (f32[128]{0:T(128)S(1)}, f32[128]{0:T(128)}, u32[]{:S(2)}) copy-start(f32[128]{0:T(128)} %param.15) | copy-start | bytes 1540
  41.5 2.6 %copy-start.7 = (f32[128]{0:T(128)S(1)}, f32[128]{0:T(128)}, u32[]{:S(2)}) copy-start(f32[128]{0:T(128)} %param.14) | copy-start | bytes 1540
  41.7 19.3 %copy-start.4 = (f32[128]{0:T(128)S(1)}, f32[128]{0:T(128)}, u32[]{:S(2)}) copy-start(f32[128]{0:T(128)} %param.20) | copy-start | bytes 1540
  41.7 19.3 %copy-start.5 = (f32[128]{0:T(128)S(1)}, f32[128]{0:T(128)}, u32[]{:S(2)}) copy-start(f32[128]{0:T(128)} %param.19) | copy-start | bytes 1540
  41.7 20.3 %copy-start.2 = (bf16[128,128]{1,0:T(8,128)(2,1)S(1)}, bf16[128,128]{1,0:T(8,128)(2,1)}, u32[]{:S(2)}) copy-start(bf16[128,128]{1,0:T(8,128)(2,1)} %param.21) | copy-start | bytes 98308
Sparse Core Ops, SparseCore 0:
  44.0 14.5 reduce-scatter.1
where the time goes:
time: 70.3 us; the launch traced here: 69.7 us
  blocking collectives  26.9 us (38%)
  waiting for transfers between devices  14.2 us (20%)
  between operations  13.6 us (19%)
  other arithmetic  6.01 us (9%)
  local copies, waits for them, and re-layouts  5.62 us (8%)
  matrix products  3.36 us (5%)
    all_gather x1, blocking collectives, shards(): lax.all_gather(right_side, 'row', axis=0, tiled=True)  26.9 us
    reduce_scatter x1, waiting for transfers between devices, shards(): lax.psum_scatter(partial_sums, 'col', scatter_dimension=1, tiled=True)  14.2 us
    all_gather x1, local copies, waits for them, and re-layouts, shards(): lax.all_gather(right_side, 'row', axis=0, tiled=True)  2.97 us
    reduce_sum x2, other arithmetic, layer_norm(): variance = jnp.mean(centred * centred, axis=-1, keepdims=True)  2.1 us
    reduce_sum x2, other arithmetic, layer_norm(): mean = jnp.mean(values, axis=-1, keepdims=True)  1.96 us
  transfers between devices with their start and end apart: 1, of which 1 were waited for; matrix products, arithmetic and copies ran while one was open for 1% of the time, Pallas kernels for 0%

commit v1 on v0

--- a/solution.py
+++ b/solution.py
@@ -1,6 +1,9 @@
+import functools
 import jax
 import jax.numpy as jnp
 from jax import lax
+from jax.experimental import pallas as pl
+from jax.experimental.pallas import tpu as pltpu
 from jax.sharding import PartitionSpec as P
 
 
@@ -62,9 +65,386 @@
     return (jax.nn.sigmoid(gate_logit) * projected).astype(jnp.bfloat16)
 
 
+MESH = pl.DeviceIdType.MESH
+
+
+def fits(rows, tile_rows, tile_cols, channels, hidden_width, cols):
+    return (
+        cols == 2
+        and rows % 4 == 0
+        and tile_rows == 8
+        and tile_cols % 16 == 0
+        and channels == 128
+        and hidden_width == 128
+        and rows * tile_rows == cols * tile_cols
+        and rows * tile_rows * tile_cols <= 4096
+    )
+
+
+def kernel(
+    rows,
+    tile_rows,
+    tile_cols,
+    pair_h,
+    mask_h,
+    chain_h,
+    in_gain_h,
+    in_shift_h,
+    out_gain_h,
+    out_shift_h,
+    w_proj_h,
+    w_gate_h,
+    bias_h,
+    w_out_h,
+    out_ref,
+    pair_v,
+    mask_v,
+    chain_v,
+    in_gain_v,
+    in_shift_v,
+    out_gain_v,
+    out_shift_v,
+    w_proj_v,
+    w_gate_v,
+    bias_v,
+    w_out_v,
+    b_own,
+    a_buf,
+    b_buf,
+    h_out,
+    h_buf,
+    a_wide,
+    b_wide,
+    sums,
+    mask_wide,
+    gate,
+    proj_s,
+    in_sem,
+    a_send,
+    a_recv,
+    b_send,
+    b_recv,
+    h_send,
+    h_recv,
+):
+    flat = tile_rows * tile_cols
+    line = rows // 2
+    half = line // 2
+    grp = lax.axis_index("grp")
+    row = lax.axis_index("row")
+    core = lax.axis_index("col")
+    z = row // 2
+    y = row % 2
+    other_y = 1 - y
+    other_core = 1 - core
+    home = z // half
+
+    copies = [
+        pltpu.make_async_copy(src, dst, in_sem.at[n])
+        for n, (src, dst) in enumerate(
+            (
+                (pair_h, pair_v),
+                (w_proj_h, w_proj_v),
+                (mask_h, mask_v),
+                (chain_h, chain_v),
+                (bias_h, bias_v),
+                (in_gain_h, in_gain_v),
+                (in_shift_h, in_shift_v),
+                (out_gain_h, out_gain_v),
+                (out_shift_h, out_shift_v),
+                (w_gate_h, w_gate_v),
+                (w_out_h, w_out_v),
+            )
+        )
+    ]
+    for copy in copies:
+        copy.start()
+    barrier = pltpu.get_barrier_semaphore()
+
+    def greet(to_row, to_core):
+        pl.semaphore_signal(
+            barrier, inc=1, device_id=(grp, to_row, to_core), device_id_type=MESH
+        )
+
+    greet(row, other_core)
+    for to_core in range(2):
+        greet(2 * z + other_y, to_core)
+        for step in range(1, line):
+            greet(2 * lax.rem(z + step, line) + y, to_core)
+
+    for copy in copies[2:9]:
+        copy.wait()
+    diagonal = lax.broadcasted_iota(jnp.int32, (tile_cols, tile_cols), 0) == lax.broadcasted_iota(
+        jnp.int32, (tile_cols, tile_cols), 1
+    )
+    for i in range(tile_rows):
+        spread = jnp.broadcast_to(
+            mask_v[pl.ds(i, 1), :].astype(jnp.float32), (tile_cols, tile_cols)
+        )
+        column = jnp.sum(jnp.where(diagonal, spread, 0.0), axis=-1, keepdims=True)
+        mask_wide[pl.ds(i * tile_cols, tile_cols), :] = jnp.broadcast_to(column, (tile_cols, 128))
+    residues = chain_v.shape[1]
+    chains = chain_v[...].astype(jnp.float32)
+    lane = lax.broadcasted_iota(jnp.int32, (tile_cols, residues), 1)
+    place = lax.broadcasted_iota(jnp.int32, (tile_cols, residues), 0) + core * tile_cols
+    col_chain = jnp.sum(
+        jnp.where(lane == place, jnp.broadcast_to(chains, (tile_cols, residues)), 0.0),
+        axis=-1,
+        keepdims=True,
+    )
+    row_lane = lax.broadcasted_iota(jnp.int32, (1, residues), 1)
+    for i in range(tile_rows):
+        row_chain = jnp.sum(
+            jnp.where(row_lane == row * tile_rows + i, chains, 0.0), axis=-1, keepdims=True
+        )
+        same = jnp.broadcast_to(col_chain == row_chain, (tile_cols, 128))
+        gate[pl.ds(i * tile_cols, tile_cols), :] = jnp.where(
+            same,
+            jnp.broadcast_to(bias_v[0:1, :], (tile_cols, 128)),
+            jnp.broadcast_to(bias_v[1:2, :], (tile_cols, 128)),
+        )
+    sums[...] = jnp.zeros_like(sums)
+
+    copies[0].wait()
+    normed = layer_norm(
+        pair_v[...].reshape(flat, 128).astype(jnp.float32), in_gain_v[...], in_shift_v[...]
+    ).astype(jnp.bfloat16)
+    copies[1].wait()
+
+    def side(start):
+        proj = jnp.dot(
+            normed, w_proj_v[:, start : start + 256], preferred_element_type=jnp.float32
+        )
+        return (mask_wide[...] * jax.nn.sigmoid(proj[:, 128:]) * proj[:, :128]).astype(
+            jnp.bfloat16
+        )
+
+    b_own[...] = side(256)
+    pl.semaphore_wait(barrier, 3 + 2 * (line - 1))
+
+    slot = (z % half) * 2 + core
+    b_copies = []
+    for step in range(1, line):
+        b_copies.append(
+            pltpu.make_async_remote_copy(
+                src_ref=b_own,
+                dst_ref=b_buf.at[slot],
+                send_sem=b_send.at[step],
+                recv_sem=b_recv.at[slot],
+                device_id=(grp, 2 * lax.rem(z + line - step, line) + y, home),
+                device_id_type=MESH,
+            )
+        )
+        b_copies[-1].start()
+    to_sibling = pltpu.make_async_remote_copy(
+        src_ref=b_own,
+        dst_ref=b_buf.at[slot],
+        send_sem=b_send.at[0],
+        recv_sem=b_recv.at[slot],
+        device_id=(grp, row, other_core),
+        device_id_type=MESH,
+    )
+
+    @pl.when(home != core)
+    def _():
+        to_sibling.start()
+
+    @pl.when(home == core)
+    def _():
+        pltpu.make_async_copy(b_own, b_buf.at[slot], b_recv.at[slot]).start()
+
+    a_own = y * 2 + core
+    a_buf[a_own] = side(0)
+    a_copies = []
+    for n, (to_row, to_core) in enumerate(
+        ((row, other_core), (2 * z + other_y, core), (2 * z + other_y, other_core))
+    ):
+        a_copies.append(
+            pltpu.make_async_remote_copy(
+                src_ref=a_buf.at[a_own],
+                dst_ref=a_buf.at[a_own],
+                send_sem=a_send.at[n],
+                recv_sem=a_recv.at[a_own],
+                device_id=(grp, to_row, to_core),
+                device_id_type=MESH,
+            )
+        )
+        a_copies[-1].start()
+
+    def widen_a(index):
+        a_wide[pl.ds(index * flat, flat), :] = a_buf[index].astype(jnp.float32)
+
+    def await_a(index):
+        pltpu.make_async_remote_copy(
+            src_ref=a_buf.at[index],
+            dst_ref=a_buf.at[index],
+            send_sem=a_send.at[0],
+            recv_sem=a_recv.at[index],
+            device_id=(grp, row, other_core),
+            device_id_type=MESH,
+        ).wait_recv()
+        widen_a(index)
+
+    def await_b(index):
+        pltpu.make_async_remote_copy(
+            src_ref=b_own,
+            dst_ref=b_buf.at[index],
+            send_sem=b_send.at[0],
+            recv_sem=b_recv.at[index],
+            device_id=(grp, row, other_core),
+            device_id_type=MESH,
+        ).wait_recv()
+        b_wide[pl.ds(index * flat, flat), :] = b_buf[index].astype(jnp.float32)
+
+    widen_a(a_own)
+    copies[9].wait()
+    gate[...] = jax.nn.sigmoid(
+        jnp.dot(normed, w_gate_v[...], preferred_element_type=jnp.float32) + gate[...]
+    )
+    copies[10].wait()
+
+    tile = tile_rows * 8
+
+    def combine(block, k_half, which):
+        a_from = (which * 2 + k_half) * flat
+        b_from = (block * 2 + k_half) * flat
+        s_from = (block * 2 + which) * tile
+
+        def body(k, totals):
+            right = b_wide[pl.ds(b_from + k, 8, stride=tile_cols), :]
+            return tuple(
+                total + a_wide[pl.ds(a_from + i * tile_cols + k, 1), :] * right
+                for i, total in enumerate(totals)
+            )
+
+        totals = tuple(sums[pl.ds(s_from + i * 8, 8), :] for i in range(tile_rows))
+        totals = lax.fori_loop(0, tile_cols, body, totals, unroll=8)
+        for i in range(tile_rows):
+            sums[pl.ds(s_from + i * 8, 8), :] = totals[i]
+
+    def hidden_of(block, which):
+        return layer_norm(
+            sums[pl.ds((block * 2 + which) * tile, tile), :], out_gain_v[...], out_shift_v[...]
+        ).astype(jnp.bfloat16)
+
+    def project(hidden, block, which):
+        projected = jnp.dot(hidden, w_out_v[...], preferred_element_type=jnp.float32)
+        for i in range(tile_rows):
+            to = pl.multiple_of(i * tile_cols + block * 16 + which * 8, 8)
+            proj_s[pl.ds(to, 8), :] = projected[i * 8 : (i + 1) * 8, :]
+
+    nearest = jnp.where(home == core, z % half, jnp.where(home > core, half - 1, 0))
+    h_copies = []
+    for step in range(half):
+        block = lax.rem(nearest + step, half)
+        for k_half in (core, other_core):
+            if step == 0:
+                await_a(other_y * 2 + k_half)
+                if k_half is other_core:
+                    await_a(y * 2 + k_half)
+            await_b(block * 2 + k_half)
+            combine(block, k_half, other_y)
+            if k_half is other_core:
+                h_out[block] = hidden_of(block, other_y)
+                h_copies.append(
+                    pltpu.make_async_remote_copy(
+                        src_ref=h_out.at[block],
+                        dst_ref=h_buf.at[block],
+                        send_sem=h_send.at[step],
+                        recv_sem=h_recv.at[block],
+                        device_id=(grp, 2 * z + other_y, core),
+                        device_id_type=MESH,
+                    )
+                )
+                h_copies[-1].start()
+            combine(block, k_half, y)
+        project(hidden_of(block, y), block, y)
+    for step in range(half):
+        block = lax.rem(nearest + step, half)
+        pltpu.make_async_remote_copy(
+            src_ref=h_out.at[block],
+            dst_ref=h_buf.at[block],
+            send_sem=h_send.at[step],
+            recv_sem=h_recv.at[block],
+            device_id=(grp, 2 * z + other_y, core),
+            device_id_type=MESH,
+        ).wait_recv()
+        project(h_buf[block], block, other_y)
+    out_ref[...] = (
+        (gate[...] * proj_s[...]).astype(jnp.bfloat16).reshape(tile_rows, tile_cols, 128)
+    )
+    for copy in b_copies + a_copies + h_copies:
+        copy.wait_send()
+
+    @pl.when(home != core)
+    def _():
+        to_sibling.wait_send()
+
+
+def fused(
+    rows,
+    pair,
+    pair_mask,
+    chain_ids,
+    norm_gain,
+    norm_shift,
+    w_proj,
+    w_gate,
+    gate_bias,
+    out_gain,
+    out_shift,
+    w_out,
+):
+    tile_rows, tile_cols, channels = pair.shape
+    flat = tile_rows * tile_cols
+    half = rows // 4
+    tile = tile_rows * 8
+    flat_rows = [v.reshape(1, -1) for v in (chain_ids, norm_gain, norm_shift, out_gain, out_shift)]
+    operands = (pair, pair_mask, *flat_rows, w_proj, w_gate, gate_bias, w_out)
+    bf16, f32 = jnp.bfloat16, jnp.float32
+    return pl.pallas_call(
+        functools.partial(kernel, rows, tile_rows, tile_cols),
+        out_shape=jax.ShapeDtypeStruct(pair.shape, bf16),
+        in_specs=[pl.BlockSpec(memory_space=pltpu.HBM)] * len(operands),
+        out_specs=pl.BlockSpec(memory_space=pltpu.VMEM),
+        scratch_shapes=[pltpu.VMEM(value.shape, value.dtype) for value in operands]
+        + [
+            pltpu.VMEM((flat, channels), bf16),
+            pltpu.VMEM((4, flat, channels), bf16),
+            pltpu.VMEM((2 * half, flat, channels), bf16),
+            pltpu.VMEM((half, tile, channels), bf16),
+            pltpu.VMEM((half, tile, channels), bf16),
+            pltpu.VMEM((4 * flat, channels), f32),
+            pltpu.VMEM((2 * half * flat, channels), f32),
+            pltpu.VMEM((2 * half * tile, channels), f32),
+            pltpu.VMEM((flat, channels), f32),
+            pltpu.VMEM((flat, channels), f32),
+            pltpu.VMEM((flat, channels), f32),
+            pltpu.SemaphoreType.DMA((11,)),
+            pltpu.SemaphoreType.DMA((3,)),
+            pltpu.SemaphoreType.DMA((4,)),
+            pltpu.SemaphoreType.DMA((rows // 2,)),
+            pltpu.SemaphoreType.DMA((2 * half,)),
+            pltpu.SemaphoreType.DMA((half,)),
+            pltpu.SemaphoreType.DMA((half,)),
+        ],
+        compiler_params=pltpu.CompilerParams(
+            collective_id=0, has_side_effects=True, vmem_limit_bytes=16 * 1024 * 1024
+        ),
+    )(*operands)
+
+
 def solution(mesh):
+    rows, cols = mesh.shape["row"], mesh.shape["col"]
+
+    def local(*blocks):
+        tile_rows, tile_cols, channels = blocks[0].shape
+        if fits(rows, tile_rows, tile_cols, channels, blocks[-1].shape[0], cols):
+            return fused(rows, *blocks)
+        return shards(*blocks)
+
     return jax.shard_map(
-        shards,
+        local,
         mesh=mesh,
         in_specs=(
             P(("grp", "row"), "col", None),

time: 70.3 us -> 21.2 us (0.30)
  blocking collectives: 26.9 us -> 0 us
  Pallas kernels: 0 us -> 16.2 us
  waiting for transfers between devices: 14.2 us -> 0 us
  between operations: 13.6 us -> 0.05 us
  other arithmetic: 6.01 us -> 0 us
  matrix products: 3.36 us -> 0 us
  local copies, waits for them, and re-layouts: 5.62 us -> 4.61 us
    all_gather x1 -> x0, blocking collectives: 26.9 us -> none  [shards(): lax.all_gather(right_side, 'row', axis=0, tiled=True)]
    pallas_call x0 -> x1, Pallas kernels: none -> 16.2 us  [fused(): pl.pallas_call(functools.partial(kernel, rows, tile_rows, tile_cols), out...]
    reduce_scatter x1 -> x0, waiting for transfers between devices: 14.2 us -> none  [shards(): lax.psum_scatter(partial_sums, 'col', scatter_dimension=1, tiled=True)]
    unnamed x18 -> x23, local copies, waits for them, and re-layouts: 0.05 us -> 4.61 us
    reduce_sum x4 -> x0, other arithmetic: 4.06 us -> none  [the longest x2 2.1 us: layer_norm(): variance = jnp.mean(centred * centred, axis=-1, keepdims=True)]
    dot_general x4 -> x0, matrix products: 3.36 us -> none  [the longest x1 1.17 us: shards(): jnp.einsum('ikc,jkc->ijc', left_side, lax.all_gather(right_side, 'row', a...]
    all_gather x1 -> x0, local copies, waits for them, and re-layouts: 2.97 us -> none  [shards(): lax.all_gather(right_side, 'row', axis=0, tiled=True)]
    convert_element_type x3 -> x0, other arithmetic: 1.85 us -> none  [the longest x1 1.05 us: shards(): hidden = layer_norm(combined, out_gain, out_shift).astype(jnp.bfloat16)]
  transfers between devices with their start and end apart: 1 -> 0, of which waited for: 1 -> 0; matrix products, arithmetic and copies ran while one was open for 1% -> 0% of each run, Pallas kernels for 0% -> 0%
where the time goes in v1:
time: 21.2 us; the launch traced here: 20.8 us
  Pallas kernels  16.2 us (76%)
  local copies, waits for them, and re-layouts  4.61 us (22%)
    pallas_call x1, Pallas kernels, fused(): pl.pallas_call(functools.partial(kernel, rows, tile_rows, tile_cols), out...  16.2 us
    unnamed x23, local copies, waits for them, and re-layouts  4.61 us

profile of v1, /device:TPU:1, one launch (start us, length us, event | category | flops | bytes accessed | tf_op | source)
XLA Modules:
  0.0 20.8 jit_solution(7274866740443354105)
XLA Ops:
  0.0 0.0 copy-start.4
  0.0 0.0 copy-start.7
  0.0 0.0 copy-start.8
  0.0 0.0 copy-start.9
  0.0 0.0 copy-start.10
  0.0 0.0 copy-start.5
  0.0 0.0 copy-start.6
  0.0 0.6 %copy-done.4 = s32[8,32]{1,0:T(8,128)S(1)} copy-done((s32[8,32]{1,0:T(8,128)S(1)}, s32[8,32]{1,0:T(8,128)}, u32[]{:S(2)}) %copy-start.4) | copy-done | bytes 1048
  0.7 0.0 copy-done.7
  0.7 0.0 copy-done.8
  0.7 0.0 copy-done.9
  0.7 0.0 copy-done.10
  0.7 0.0 copy-done.5
  0.8 0.0 copy-done.6
  0.8 0.0 copy-start
  0.8 0.9 %copy-done = bf16[128,512]{1,0:T(8,128)(2,1)S(1)} copy-done((bf16[128,512]{1,0:T(8,128)(2,1)S(1)}, bf16[128,512]{1,0:T(8,128)(2,1)}, u32[]{:S(2)}) %copy-start) | copy-done | bytes 131096
  1.7 0.0 copy-start.1
  1.7 0.8 %copy-done.1 = bf16[8,32,128]{2,1,0:T(8,128)(2,1)S(1)} copy-done((bf16[8,32,128]{2,1,0:T(8,128)(2,1)S(1)}, bf16[8,32,128]{2,1,0:T(8,128)(2,1)}, u32[]{:S(2)}) %copy-start.1) | copy-done | bytes 65560
  2.5 0.0 copy-start.2
  2.5 0.8 %copy-done.2 = bf16[128,128]{1,0:T(8,128)(2,1)S(1)} copy-done((bf16[128,128]{1,0:T(8,128)(2,1)S(1)}, bf16[128,128]{1,0:T(8,128)(2,1)}, u32[]{:S(2)}) %copy-start.2) | copy-done | bytes 32792
  3.3 0.0 copy-start.3
  3.3 0.8 %copy-done.3 = bf16[128,128]{1,0:T(8,128)(2,1)S(1)} copy-done((bf16[128,128]{1,0:T(8,128)(2,1)S(1)}, bf16[128,128]{1,0:T(8,128)(2,1)}, u32[]{:S(2)}) %copy-start.3) | copy-done | bytes 32792
  4.0 16.2 %shard_map.109 = bf16[8,32,128]{2,1,0:T(8,128)(2,1)S(1)} custom-call(bf16[8,32,128]{2,1,0:T(8,128)(2,1)S(1)} %copy-done.1, s32[8,32]{1,0:T(8,128)S(1)} %copy-done.4, s32[1,64]{1,0:T(1,128)S(1)} %bitcast.5, f32[1,128]{1,0:T(1,128)S(1)} %bitcast.6, f32[1,128]{1,0:T(1,128)S(1)} %bitcast.7, f32[1,128]{1,0:T(1,128)S(1)} %bitcast.8, f32[1,128]{1,0:T(1,128)S(1)} %bitcast.9, ...), custom_call_target="tpu_custom_call" | custom-call | tf_op jit(solution)/shard_map/pallas_call | solution.py:405
  20.2 0.6 %copy.13 = bf16[8,32,128]{2,1,0:T(8,128)(2,1)} copy(bf16[8,32,128]{2,1,0:T(8,128)(2,1)S(1)} %shard_map.109) | data formatting | bytes 131072
Async XLA Ops:
  0.0 0.7 %copy-start.4 = (s32[8,32]{1,0:T(8,128)S(1)}, s32[8,32]{1,0:T(8,128)}, u32[]{:S(2)}) copy-start(s32[8,32]{1,0:T(8,128)} %mask_h.1) | copy-start | bytes 3076
  0.0 0.7 %copy-start.7 = (f32[128]{0:T(128)S(1)}, f32[128]{0:T(128)}, u32[]{:S(2)}) copy-start(f32[128]{0:T(128)} %param.14) | copy-start | bytes 1540
  0.0 0.7 %copy-start.8 = (f32[128]{0:T(128)S(1)}, f32[128]{0:T(128)}, u32[]{:S(2)}) copy-start(f32[128]{0:T(128)} %param.15) | copy-start | bytes 1540
  0.0 0.7 %copy-start.9 = (f32[128]{0:T(128)S(1)}, f32[128]{0:T(128)}, u32[]{:S(2)}) copy-start(f32[128]{0:T(128)} %param.19) | copy-start | bytes 1540
  0.0 0.7 %copy-start.10 = (f32[128]{0:T(128)S(1)}, f32[128]{0:T(128)}, u32[]{:S(2)}) copy-start(f32[128]{0:T(128)} %param.20) | copy-start | bytes 1540
  0.0 0.7 %copy-start.5 = (f32[2,128]{1,0:T(2,128)S(1)}, f32[2,128]{1,0:T(2,128)}, u32[]{:S(2)}) copy-start(f32[2,128]{1,0:T(2,128)} %bias_h.1) | copy-start | bytes 3076
  0.0 0.7 %copy-start.6 = (s32[64]{0:T(128)S(1)}, s32[64]{0:T(128)}, u32[]{:S(2)}) copy-start(s32[64]{0:T(128)} %param.13) | copy-start | bytes 772
  0.8 0.9 %copy-start = (bf16[128,512]{1,0:T(8,128)(2,1)S(1)}, bf16[128,512]{1,0:T(8,128)(2,1)}, u32[]{:S(2)}) copy-start(bf16[128,512]{1,0:T(8,128)(2,1)} %w_proj_h.1) | copy-start | bytes 393220
  1.7 0.8 %copy-start.1 = (bf16[8,32,128]{2,1,0:T(8,128)(2,1)S(1)}, bf16[8,32,128]{2,1,0:T(8,128)(2,1)}, u32[]{:S(2)}) copy-start(bf16[8,32,128]{2,1,0:T(8,128)(2,1)} %pair_h.1) | copy-start | bytes 196612
  2.5 0.8 %copy-start.2 = (bf16[128,128]{1,0:T(8,128)(2,1)S(1)}, bf16[128,128]{1,0:T(8,128)(2,1)}, u32[]{:S(2)}) copy-start(bf16[128,128]{1,0:T(8,128)(2,1)} %w_gate_h.1) | copy-start | bytes 98308
  3.3 0.8 %copy-start.3 = (bf16[128,128]{1,0:T(8,128)(2,1)S(1)}, bf16[128,128]{1,0:T(8,128)(2,1)}, u32[]{:S(2)}) copy-start(bf16[128,128]{1,0:T(8,128)(2,1)} %w_out_h.1) | copy-start | bytes 98308

commit v2 on v1

--- a/solution.py
+++ b/solution.py
@@ -429,7 +429,7 @@
             pltpu.SemaphoreType.DMA((half,)),
         ],
         compiler_params=pltpu.CompilerParams(
-            collective_id=0, has_side_effects=True, vmem_limit_bytes=16 * 1024 * 1024
+            collective_id=0, has_side_effects=True, vmem_limit_bytes=60 * 1024 * 1024
         ),
     )(*operands)
 

time: 21.2 us -> 18.1 us (0.85); the launches traced: 20.8 us -> 18 us
  local copies, waits for them, and re-layouts: 4.61 us -> 1.47 us
  Pallas kernels: 16.2 us -> 16.5 us
    unnamed x23 -> x1, local copies, waits for them, and re-layouts: 4.61 us -> 1.47 us
    pallas_call x1, Pallas kernels: 16.2 us -> 16.5 us  [fused(): pl.pallas_call(functools.partial(kernel, rows, tile_rows, tile_cols), out...]
where the time goes in v2:
time: 18.1 us; the launch traced here: 18 us
  Pallas kernels  16.5 us (91%)
  local copies, waits for them, and re-layouts  1.47 us (8%)
    pallas_call x1, Pallas kernels, fused(): pl.pallas_call(functools.partial(kernel, rows, tile_rows, tile_cols), out...  16.5 us
    unnamed x1, local copies, waits for them, and re-layouts  1.47 us

profile of v2, /device:TPU:1, one launch (start us, length us, event | category | flops | bytes accessed | tf_op | source)
XLA Modules:
  0.0 18.0 jit_solution(18008357974547838906)
XLA Ops:
  0.0 16.5 %shard_map.109 = bf16[8,32,128]{2,1,0:T(8,128)(2,1)} custom-call(bf16[8,32,128]{2,1,0:T(8,128)(2,1)} %pair_h.1, s32[8,32]{1,0:T(8,128)} %mask_h.1, s32[1,64]{1,0:T(1,128)} %bitcast.5, f32[1,128]{1,0:T(1,128)} %bitcast.6, f32[1,128]{1,0:T(1,128)} %bitcast.7, f32[1,128]{1,0:T(1,128)} %bitcast.8, f32[1,128]{1,0:T(1,128)} %bitcast.9, bf16[128,512]{1,0:T(8,128)(2,1)} %w_proj_h.1, ...), custom_call_target="tpu_custom_call" | custom-call | tf_op jit(solution)/shard_map/pallas_call | solution.py:405
  16.5 1.5 %copy.13 = bf16[8,32,128]{2,1,0:T(8,128)(2,1)} copy(bf16[8,32,128]{2,1,0:T(8,128)(2,1)} %shard_map.109) | data formatting | bytes 131072

commit v3 on v1

--- a/solution.py
+++ b/solution.py
@@ -431,7 +431,7 @@
         compiler_params=pltpu.CompilerParams(
             collective_id=0, has_side_effects=True, vmem_limit_bytes=16 * 1024 * 1024
         ),
-    )(*operands)
+    )(*[pltpu.with_memory_space_constraint(value, pltpu.HBM) for value in operands])
 
 
 def solution(mesh):

time: 21.2 us -> 16.7 us (0.79)
  local copies, waits for them, and re-layouts: 4.61 us -> 0.63 us
  Pallas kernels: 16.2 us -> 15.9 us
    unnamed x23 -> x1, local copies, waits for them, and re-layouts: 4.61 us -> 0.63 us
    pallas_call x1, Pallas kernels: 16.2 us -> 15.9 us  [fused(): pl.pallas_call(functools.partial(kernel, rows, tile_rows, tile_cols), out...]
where the time goes in v3:
time: 16.7 us; the launch traced here: 16.5 us
  Pallas kernels  15.9 us (95%)
  local copies, waits for them, and re-layouts  0.63 us (4%)
    pallas_call x1, Pallas kernels, fused(): pl.pallas_call(functools.partial(kernel, rows, tile_rows, tile_cols), out...  15.9 us
    unnamed x1, local copies, waits for them, and re-layouts  0.63 us

profile of v3, /device:TPU:1, one launch (start us, length us, event | category | flops | bytes accessed | tf_op | source)
XLA Modules:
  0.0 16.5 jit_solution(18393934585702604446)
XLA Ops:
  0.0 15.9 %shard_map.109 = bf16[8,32,128]{2,1,0:T(8,128)(2,1)S(1)} custom-call(bf16[8,32,128]{2,1,0:T(8,128)(2,1)} %pair_h.1, s32[8,32]{1,0:T(8,128)} %mask_h.1, s32[1,64]{1,0:T(1,128)} %bitcast.5, f32[1,128]{1,0:T(1,128)} %bitcast.6, f32[1,128]{1,0:T(1,128)} %bitcast.7, f32[1,128]{1,0:T(1,128)} %bitcast.8, f32[1,128]{1,0:T(1,128)} %bitcast.9, ...), custom_call_target="tpu_custom_call" | custom-call | tf_op jit(solution)/shard_map/pallas_call | solution.py:405
  15.9 0.6 %copy.13 = bf16[8,32,128]{2,1,0:T(8,128)(2,1)} copy(bf16[8,32,128]{2,1,0:T(8,128)(2,1)S(1)} %shard_map.109) | data formatting | bytes 131072

commit v4 on v3

--- a/solution.py
+++ b/solution.py
@@ -71,7 +71,7 @@
 def fits(rows, tile_rows, tile_cols, channels, hidden_width, cols):
     return (
         cols == 2
-        and rows % 4 == 0
+        and rows == 8
         and tile_rows == 8
         and tile_cols % 16 == 0
         and channels == 128
@@ -124,6 +124,7 @@
     a_recv,
     b_send,
     b_recv,
+    relay_send,
     h_send,
     h_recv,
 ):
@@ -138,6 +139,27 @@
     other_y = 1 - y
     other_core = 1 - core
     home = z // half
+
+    barrier = pltpu.get_barrier_semaphore()
+
+    def greet(to_row, to_core):
+        pl.semaphore_signal(
+            barrier, inc=1, device_id=(grp, to_row, to_core), device_id_type=MESH
+        )
+
+    near, far, across = z + 1 - 2 * (z % 2), lax.rem(z + 2, 4), 3 - z
+    inner = jnp.logical_or(z == 1, z == 2)
+    for to_core in range(2):
+        greet(2 * far + y, to_core)
+    for to_core in range(2):
+        greet(2 * near + y, to_core)
+        greet(2 * z + other_y, to_core)
+    greet(row, other_core)
+
+    @pl.when(inner)
+    def _():
+        for to_core in range(2):
+            greet(2 * across + y, to_core)
 
     copies = [
         pltpu.make_async_copy(src, dst, in_sem.at[n])
@@ -159,19 +181,6 @@
     ]
     for copy in copies:
         copy.start()
-    barrier = pltpu.get_barrier_semaphore()
-
-    def greet(to_row, to_core):
-        pl.semaphore_signal(
-            barrier, inc=1, device_id=(grp, to_row, to_core), device_id_type=MESH
-        )
-
-    greet(row, other_core)
-    for to_core in range(2):
-        greet(2 * z + other_y, to_core)
-        for step in range(1, line):
-            greet(2 * lax.rem(z + step, line) + y, to_core)
-
     for copy in copies[2:9]:
         copy.wait()
     diagonal = lax.broadcasted_iota(jnp.int32, (tile_cols, tile_cols), 0) == lax.broadcasted_iota(
@@ -220,22 +229,38 @@
         )
 
     b_own[...] = side(256)
-    pl.semaphore_wait(barrier, 3 + 2 * (line - 1))
+    a_own = y * 2 + core
+    a_left = side(0)
+    a_buf[a_own] = a_left
+    a_wide[pl.ds(a_own * flat, flat), :] = a_left.astype(jnp.float32)
+    copies[9].wait()
+    gate[...] = jax.nn.sigmoid(
+        jnp.dot(normed, w_gate_v[...], preferred_element_type=jnp.float32) + gate[...]
+    )
+    copies[10].wait()
+    pl.semaphore_wait(barrier, jnp.where(inner, 9, 7))
 
     slot = (z % half) * 2 + core
-    b_copies = []
-    for step in range(1, line):
-        b_copies.append(
-            pltpu.make_async_remote_copy(
-                src_ref=b_own,
-                dst_ref=b_buf.at[slot],
-                send_sem=b_send.at[step],
-                recv_sem=b_recv.at[slot],
-                device_id=(grp, 2 * lax.rem(z + line - step, line) + y, home),
-                device_id_type=MESH,
-            )
-        )
-        b_copies[-1].start()
+
+    def b_copy(n, to_z):
+        return pltpu.make_async_remote_copy(
+            src_ref=b_own,
+            dst_ref=b_buf.at[slot],
+            send_sem=b_send.at[n],
+            recv_sem=b_recv.at[slot],
+            device_id=(grp, 2 * to_z + y, home),
+            device_id_type=MESH,
+        )
+
+    to_across = b_copy(1, across)
+    b_copies = [b_copy(2, far), b_copy(3, near)]
+    b_copies[0].start()
+
+    @pl.when(inner)
+    def _():
+        to_across.start()
+
+    b_copies[1].start()
     to_sibling = pltpu.make_async_remote_copy(
         src_ref=b_own,
         dst_ref=b_buf.at[slot],
@@ -253,8 +278,6 @@
     def _():
         pltpu.make_async_copy(b_own, b_buf.at[slot], b_recv.at[slot]).start()
 
-    a_own = y * 2 + core
-    a_buf[a_own] = side(0)
     a_copies = []
     for n, (to_row, to_core) in enumerate(
         ((row, other_core), (2 * z + other_y, core), (2 * z + other_y, other_core))
@@ -286,22 +309,38 @@
         widen_a(index)
 
     def await_b(index):
-        pltpu.make_async_remote_copy(
-            src_ref=b_own,
-            dst_ref=b_buf.at[index],
-            send_sem=b_send.at[0],
-            recv_sem=b_recv.at[index],
-            device_id=(grp, row, other_core),
+        @pl.when(jnp.logical_not(jnp.logical_and(relays, index // 2 == far % half)))
+        def _():
+            pltpu.make_async_remote_copy(
+                src_ref=b_own,
+                dst_ref=b_buf.at[index],
+                send_sem=b_send.at[0],
+                recv_sem=b_recv.at[index],
+                device_id=(grp, row, other_core),
+                device_id_type=MESH,
+            ).wait_recv()
+
+        b_wide[pl.ds(index * flat, flat), :] = b_buf[index].astype(jnp.float32)
+
+    relays = jnp.logical_and(inner, home != core)
+
+    def relay_copy(k_half):
+        passed = (far % half) * 2 + k_half
+        return pltpu.make_async_remote_copy(
+            src_ref=b_buf.at[passed],
+            dst_ref=b_buf.at[passed],
+            send_sem=relay_send.at[k_half],
+            recv_sem=b_recv.at[passed],
+            device_id=(grp, 2 * near + y, core),
             device_id_type=MESH,
-        ).wait_recv()
-        b_wide[pl.ds(index * flat, flat), :] = b_buf[index].astype(jnp.float32)
-
-    widen_a(a_own)
-    copies[9].wait()
-    gate[...] = jax.nn.sigmoid(
-        jnp.dot(normed, w_gate_v[...], preferred_element_type=jnp.float32) + gate[...]
-    )
-    copies[10].wait()
+        )
+
+    @pl.when(relays)
+    def _():
+        for k_half in range(2):
+            passing = relay_copy(k_half)
+            passing.wait_recv()
+            passing.start()
 
     tile = tile_rows * 8
 
@@ -379,6 +418,15 @@
     @pl.when(home != core)
     def _():
         to_sibling.wait_send()
+
+    @pl.when(inner)
+    def _():
+        to_across.wait_send()
+
+    @pl.when(relays)
+    def _():
+        for k_half in range(2):
+            relay_copy(k_half).wait_send()
 
 
 def fused(
@@ -423,8 +471,9 @@
             pltpu.SemaphoreType.DMA((11,)),
             pltpu.SemaphoreType.DMA((3,)),
             pltpu.SemaphoreType.DMA((4,)),
-            pltpu.SemaphoreType.DMA((rows // 2,)),
+            pltpu.SemaphoreType.DMA((4,)),
             pltpu.SemaphoreType.DMA((2 * half,)),
+            pltpu.SemaphoreType.DMA((2,)),
             pltpu.SemaphoreType.DMA((half,)),
             pltpu.SemaphoreType.DMA((half,)),
         ],

time: 16.7 us -> 15.7 us (0.940)
  Pallas kernels: 15.9 us -> 14.9 us
    pallas_call x1, Pallas kernels: 15.9 us -> 14.9 us  [fused(): pl.pallas_call(functools.partial(kernel, rows, tile_rows, tile_cols), out...]
where the time goes in v4:
time: 15.7 us; the launch traced here: 15.5 us
  Pallas kernels  14.9 us (95%)
  local copies, waits for them, and re-layouts  0.63 us (4%)
    pallas_call x1, Pallas kernels, fused(): pl.pallas_call(functools.partial(kernel, rows, tile_rows, tile_cols), out...  14.9 us
    unnamed x1, local copies, waits for them, and re-layouts  0.63 us

profile of v4, /device:TPU:1, one launch (start us, length us, event | category | flops | bytes accessed | tf_op | source)
XLA Modules:
  0.0 15.5 jit_solution(17941727709030601181)
XLA Ops:
  0.0 14.9 %shard_map.109 = bf16[8,32,128]{2,1,0:T(8,128)(2,1)S(1)} custom-call(bf16[8,32,128]{2,1,0:T(8,128)(2,1)} %pair_h.1, s32[8,32]{1,0:T(8,128)} %mask_h.1, s32[1,64]{1,0:T(1,128)} %bitcast.5, f32[1,128]{1,0:T(1,128)} %bitcast.6, f32[1,128]{1,0:T(1,128)} %bitcast.7, f32[1,128]{1,0:T(1,128)} %bitcast.8, f32[1,128]{1,0:T(1,128)} %bitcast.9, ...), custom_call_target="tpu_custom_call" | custom-call | tf_op jit(solution)/shard_map/pallas_call | solution.py:453
  14.9 0.6 %copy.13 = bf16[8,32,128]{2,1,0:T(8,128)(2,1)} copy(bf16[8,32,128]{2,1,0:T(8,128)(2,1)S(1)} %shard_map.109) | data formatting | bytes 131072

commit v5 on v4

--- a/solution.py
+++ b/solution.py
@@ -66,6 +66,7 @@
 
 
 MESH = pl.DeviceIdType.MESH
+PIECES = 4
 
 
 def fits(rows, tile_rows, tile_cols, channels, hidden_width, cols):
@@ -241,42 +242,54 @@
     pl.semaphore_wait(barrier, jnp.where(inner, 9, 7))
 
     slot = (z % half) * 2 + core
-
-    def b_copy(n, to_z):
-        return pltpu.make_async_remote_copy(
-            src_ref=b_own,
-            dst_ref=b_buf.at[slot],
-            send_sem=b_send.at[n],
-            recv_sem=b_recv.at[slot],
-            device_id=(grp, 2 * to_z + y, home),
-            device_id_type=MESH,
-        )
-
-    to_across = b_copy(1, across)
-    b_copies = [b_copy(2, far), b_copy(3, near)]
-    b_copies[0].start()
+    piece = flat // PIECES
+
+    def piece_of(ref, n):
+        return ref.at[pl.ds(n * piece, piece)]
+
+    def b_copies_to(n, to_row):
+        return [
+            pltpu.make_async_remote_copy(
+                src_ref=piece_of(b_own, p),
+                dst_ref=piece_of(b_buf.at[slot], p),
+                send_sem=b_send.at[n * PIECES + p],
+                recv_sem=b_recv.at[slot * PIECES + p],
+                device_id=(grp, to_row, other_core if n == 0 else home),
+                device_id_type=MESH,
+            )
+            for p in range(PIECES)
+        ]
+
+    to_sibling = b_copies_to(0, row)
+    to_across = b_copies_to(1, 2 * across + y)
+    to_far = b_copies_to(2, 2 * far + y)
+    to_near = b_copies_to(3, 2 * near + y)
+
+    def start(group):
+        for copy in group:
+            copy.start()
 
     @pl.when(inner)
     def _():
-        to_across.start()
-
-    b_copies[1].start()
-    to_sibling = pltpu.make_async_remote_copy(
-        src_ref=b_own,
-        dst_ref=b_buf.at[slot],
-        send_sem=b_send.at[0],
-        recv_sem=b_recv.at[slot],
-        device_id=(grp, row, other_core),
-        device_id_type=MESH,
-    )
+        start(to_near)
+        start(to_far)
+        start(to_across)
+
+    @pl.when(jnp.logical_not(inner))
+    def _():
+        start(to_far)
+        start(to_near)
 
     @pl.when(home != core)
     def _():
-        to_sibling.start()
+        start(to_sibling)
 
     @pl.when(home == core)
     def _():
-        pltpu.make_async_copy(b_own, b_buf.at[slot], b_recv.at[slot]).start()
+        for p in range(PIECES):
+            pltpu.make_async_copy(
+                piece_of(b_own, p), piece_of(b_buf.at[slot], p), b_recv.at[slot * PIECES + p]
+            ).start()
 
     a_copies = []
     for n, (to_row, to_core) in enumerate(
@@ -311,36 +324,38 @@
     def await_b(index):
         @pl.when(jnp.logical_not(jnp.logical_and(relays, index // 2 == far % half)))
         def _():
-            pltpu.make_async_remote_copy(
-                src_ref=b_own,
-                dst_ref=b_buf.at[index],
-                send_sem=b_send.at[0],
-                recv_sem=b_recv.at[index],
-                device_id=(grp, row, other_core),
-                device_id_type=MESH,
-            ).wait_recv()
+            for p in range(PIECES):
+                pltpu.make_async_remote_copy(
+                    src_ref=piece_of(b_own, p),
+                    dst_ref=piece_of(b_buf.at[index], p),
+                    send_sem=b_send.at[p],
+                    recv_sem=b_recv.at[index * PIECES + p],
+                    device_id=(grp, row, other_core),
+                    device_id_type=MESH,
+                ).wait_recv()
 
         b_wide[pl.ds(index * flat, flat), :] = b_buf[index].astype(jnp.float32)
 
     relays = jnp.logical_and(inner, home != core)
 
-    def relay_copy(k_half):
+    def relay_copy(k_half, p):
         passed = (far % half) * 2 + k_half
         return pltpu.make_async_remote_copy(
-            src_ref=b_buf.at[passed],
-            dst_ref=b_buf.at[passed],
-            send_sem=relay_send.at[k_half],
-            recv_sem=b_recv.at[passed],
+            src_ref=piece_of(b_buf.at[passed], p),
+            dst_ref=piece_of(b_buf.at[passed], p),
+            send_sem=relay_send.at[k_half * PIECES + p],
+            recv_sem=b_recv.at[passed * PIECES + p],
             device_id=(grp, 2 * near + y, core),
             device_id_type=MESH,
         )
 
     @pl.when(relays)
     def _():
-        for k_half in range(2):
-            passing = relay_copy(k_half)
-            passing.wait_recv()
-            passing.start()
+        for p in range(PIECES):
+            for k_half in range(2):
+                passing = relay_copy(k_half, p)
+                passing.wait_recv()
+                passing.start()
 
     tile = tile_rows * 8
 
@@ -412,21 +427,24 @@
     out_ref[...] = (
         (gate[...] * proj_s[...]).astype(jnp.bfloat16).reshape(tile_rows, tile_cols, 128)
     )
-    for copy in b_copies + a_copies + h_copies:
+    for copy in to_far + to_near + a_copies + h_copies:
         copy.wait_send()
 
     @pl.when(home != core)
     def _():
-        to_sibling.wait_send()
+        for copy in to_sibling:
+            copy.wait_send()
 
     @pl.when(inner)
     def _():
-        to_across.wait_send()
+        for copy in to_across:
+            copy.wait_send()
 
     @pl.when(relays)
     def _():
-        for k_half in range(2):
-            relay_copy(k_half).wait_send()
+        for p in range(PIECES):
+            for k_half in range(2):
+                relay_copy(k_half, p).wait_send()
 
 
 def fused(
@@ -471,9 +489,9 @@
             pltpu.SemaphoreType.DMA((11,)),
             pltpu.SemaphoreType.DMA((3,)),
             pltpu.SemaphoreType.DMA((4,)),
-            pltpu.SemaphoreType.DMA((4,)),
-            pltpu.SemaphoreType.DMA((2 * half,)),
-            pltpu.SemaphoreType.DMA((2,)),
+            pltpu.SemaphoreType.DMA((4 * PIECES,)),
+            pltpu.SemaphoreType.DMA((2 * half * PIECES,)),
+            pltpu.SemaphoreType.DMA((2 * PIECES,)),
             pltpu.SemaphoreType.DMA((half,)),
             pltpu.SemaphoreType.DMA((half,)),
         ],

time: 15.7 us -> 15.1 us (0.962)
  Pallas kernels: 14.9 us -> 14.4 us
    pallas_call x1, Pallas kernels: 14.9 us -> 14.4 us  [fused(): pl.pallas_call(functools.partial(kernel, rows, tile_rows, tile_cols), out...]
where the time goes in v5:
time: 15.1 us; the launch traced here: 15 us
  Pallas kernels  14.4 us (95%)
  local copies, waits for them, and re-layouts  0.63 us (4%)
    pallas_call x1, Pallas kernels, fused(): pl.pallas_call(functools.partial(kernel, rows, tile_rows, tile_cols), out...  14.4 us
    unnamed x1, local copies, waits for them, and re-layouts  0.63 us

profile of v5, /device:TPU:1, one launch (start us, length us, event | category | flops | bytes accessed | tf_op | source)
XLA Modules:
  0.0 15.0 jit_solution(4410031638610071020)
XLA Ops:
  0.0 14.4 %shard_map.109 = bf16[8,32,128]{2,1,0:T(8,128)(2,1)S(1)} custom-call(bf16[8,32,128]{2,1,0:T(8,128)(2,1)} %pair_h.1, s32[8,32]{1,0:T(8,128)} %mask_h.1, s32[1,64]{1,0:T(1,128)} %bitcast.5, f32[1,128]{1,0:T(1,128)} %bitcast.6, f32[1,128]{1,0:T(1,128)} %bitcast.7, f32[1,128]{1,0:T(1,128)} %bitcast.8, f32[1,128]{1,0:T(1,128)} %bitcast.9, ...), custom_call_target="tpu_custom_call" | custom-call | tf_op jit(solution)/shard_map/pallas_call | solution.py:471
  14.4 0.6 %copy.13 = bf16[8,32,128]{2,1,0:T(8,128)(2,1)} copy(bf16[8,32,128]{2,1,0:T(8,128)(2,1)S(1)} %shard_map.109) | data formatting | bytes 131072

commit v6 on v5

--- a/solution.py
+++ b/solution.py
@@ -150,17 +150,28 @@
 
     near, far, across = z + 1 - 2 * (z % 2), lax.rem(z + 2, 4), 3 - z
     inner = jnp.logical_or(z == 1, z == 2)
+    @pl.when(home != core)
+    def _():
+        for to_core in range(2):
+            greet(2 * far + y, to_core)
+
+        @pl.when(inner)
+        def _():
+            for to_core in range(2):
+                greet(2 * across + y, to_core)
+
+        @pl.when(jnp.logical_not(inner))
+        def _():
+            greet(2 * near + y, core)
+
+    @pl.when(home == core)
+    def _():
+        for to_core in range(2):
+            greet(2 * near + y, to_core)
+
     for to_core in range(2):
-        greet(2 * far + y, to_core)
-    for to_core in range(2):
-        greet(2 * near + y, to_core)
         greet(2 * z + other_y, to_core)
     greet(row, other_core)
-
-    @pl.when(inner)
-    def _():
-        for to_core in range(2):
-            greet(2 * across + y, to_core)
 
     copies = [
         pltpu.make_async_copy(src, dst, in_sem.at[n])
@@ -239,7 +250,7 @@
         jnp.dot(normed, w_gate_v[...], preferred_element_type=jnp.float32) + gate[...]
     )
     copies[10].wait()
-    pl.semaphore_wait(barrier, jnp.where(inner, 9, 7))
+    pl.semaphore_wait(barrier, 5 + jnp.where(inner, jnp.where(home != core, 2, 1), 0))
 
     slot = (z % half) * 2 + core
     piece = flat // PIECES
@@ -247,49 +258,51 @@
     def piece_of(ref, n):
         return ref.at[pl.ds(n * piece, piece)]
 
-    def b_copies_to(n, to_row):
-        return [
-            pltpu.make_async_remote_copy(
-                src_ref=piece_of(b_own, p),
-                dst_ref=piece_of(b_buf.at[slot], p),
-                send_sem=b_send.at[n * PIECES + p],
-                recv_sem=b_recv.at[slot * PIECES + p],
-                device_id=(grp, to_row, other_core if n == 0 else home),
-                device_id_type=MESH,
-            )
-            for p in range(PIECES)
-        ]
-
-    to_sibling = b_copies_to(0, row)
-    to_across = b_copies_to(1, 2 * across + y)
-    to_far = b_copies_to(2, 2 * far + y)
-    to_near = b_copies_to(3, 2 * near + y)
-
-    def start(group):
-        for copy in group:
+    def b_copy_to(n, to_row, to_core):
+        return pltpu.make_async_remote_copy(
+            src_ref=b_own,
+            dst_ref=b_buf.at[slot],
+            send_sem=b_send.at[n],
+            recv_sem=b_recv.at[slot * PIECES],
+            device_id=(grp, to_row, to_core),
+            device_id_type=MESH,
+        )
+
+    to_sibling = b_copy_to(0, row, other_core)
+    to_across = b_copy_to(1, 2 * across + y, home)
+    to_far = b_copy_to(2, 2 * far + y, home)
+    to_near = b_copy_to(3, 2 * near + y, home)
+    to_far_pieces = [
+        pltpu.make_async_remote_copy(
+            src_ref=piece_of(b_own, p),
+            dst_ref=piece_of(b_buf.at[slot], p),
+            send_sem=b_send.at[4 + p],
+            recv_sem=b_recv.at[slot * PIECES + p],
+            device_id=(grp, 2 * far + y, home),
+            device_id_type=MESH,
+        )
+        for p in range(PIECES)
+    ]
+
+    @pl.when(inner)
+    def _():
+        to_near.start()
+        to_far.start()
+        to_across.start()
+
+    @pl.when(jnp.logical_not(inner))
+    def _():
+        for copy in to_far_pieces:
             copy.start()
-
-    @pl.when(inner)
-    def _():
-        start(to_near)
-        start(to_far)
-        start(to_across)
-
-    @pl.when(jnp.logical_not(inner))
-    def _():
-        start(to_far)
-        start(to_near)
+        to_near.start()
 
     @pl.when(home != core)
     def _():
-        start(to_sibling)
+        to_sibling.start()
 
     @pl.when(home == core)
     def _():
-        for p in range(PIECES):
-            pltpu.make_async_copy(
-                piece_of(b_own, p), piece_of(b_buf.at[slot], p), b_recv.at[slot * PIECES + p]
-            ).start()
+        pltpu.make_async_copy(b_own, b_buf.at[slot], b_recv.at[slot * PIECES]).start()
 
     a_copies = []
     for n, (to_row, to_core) in enumerate(
@@ -322,17 +335,26 @@
         widen_a(index)
 
     def await_b(index):
-        @pl.when(jnp.logical_not(jnp.logical_and(relays, index // 2 == far % half)))
+        passed_on = jnp.logical_and(home != core, index // 2 == jnp.where(inner, far, across) % half)
+
+        def awaited(ref, n):
+            return pltpu.make_async_remote_copy(
+                src_ref=ref(b_own),
+                dst_ref=ref(b_buf.at[index]),
+                send_sem=b_send.at[0],
+                recv_sem=b_recv.at[index * PIECES + n],
+                device_id=(grp, row, other_core),
+                device_id_type=MESH,
+            )
+
+        @pl.when(jnp.logical_not(passed_on))
+        def _():
+            awaited(lambda ref: ref, 0).wait_recv()
+
+        @pl.when(jnp.logical_and(passed_on, jnp.logical_not(inner)))
         def _():
             for p in range(PIECES):
-                pltpu.make_async_remote_copy(
-                    src_ref=piece_of(b_own, p),
-                    dst_ref=piece_of(b_buf.at[index], p),
-                    send_sem=b_send.at[p],
-                    recv_sem=b_recv.at[index * PIECES + p],
-                    device_id=(grp, row, other_core),
-                    device_id_type=MESH,
-                ).wait_recv()
+                awaited(lambda ref: piece_of(ref, p), p).wait_recv()
 
         b_wide[pl.ds(index * flat, flat), :] = b_buf[index].astype(jnp.float32)
 
@@ -427,17 +449,21 @@
     out_ref[...] = (
         (gate[...] * proj_s[...]).astype(jnp.bfloat16).reshape(tile_rows, tile_cols, 128)
     )
-    for copy in to_far + to_near + a_copies + h_copies:
+    for copy in [to_near] + a_copies + h_copies:
         copy.wait_send()
 
     @pl.when(home != core)
     def _():
-        for copy in to_sibling:
-            copy.wait_send()
+        to_sibling.wait_send()
 
     @pl.when(inner)
     def _():
-        for copy in to_across:
+        to_across.wait_send()
+        to_far.wait_send()
+
+    @pl.when(jnp.logical_not(inner))
+    def _():
+        for copy in to_far_pieces:
             copy.wait_send()
 
     @pl.when(relays)
@@ -489,7 +515,7 @@
             pltpu.SemaphoreType.DMA((11,)),
             pltpu.SemaphoreType.DMA((3,)),
             pltpu.SemaphoreType.DMA((4,)),
-            pltpu.SemaphoreType.DMA((4 * PIECES,)),
+            pltpu.SemaphoreType.DMA((4 + PIECES,)),
             pltpu.SemaphoreType.DMA((2 * half * PIECES,)),
             pltpu.SemaphoreType.DMA((2 * PIECES,)),
             pltpu.SemaphoreType.DMA((half,)),

time: 15.1 us -> 15 us (level)
  no operation moved by 1% of the time
where the time goes in v6:
time: 15 us; the launch traced here: 14.9 us
  Pallas kernels  14.3 us (95%)
  local copies, waits for them, and re-layouts  0.63 us (4%)
    pallas_call x1, Pallas kernels, fused(): pl.pallas_call(functools.partial(kernel, rows, tile_rows, tile_cols), out...  14.3 us
    unnamed x1, local copies, waits for them, and re-layouts  0.63 us

profile of v6, /device:TPU:1, one launch (start us, length us, event | category | flops | bytes accessed | tf_op | source)
XLA Modules:
  0.0 14.9 jit_solution(5973085051647967338)
XLA Ops:
  0.0 14.3 %shard_map.109 = bf16[8,32,128]{2,1,0:T(8,128)(2,1)S(1)} custom-call(bf16[8,32,128]{2,1,0:T(8,128)(2,1)} %pair_h.1, s32[8,32]{1,0:T(8,128)} %mask_h.1, s32[1,64]{1,0:T(1,128)} %bitcast.5, f32[1,128]{1,0:T(1,128)} %bitcast.6, f32[1,128]{1,0:T(1,128)} %bitcast.7, f32[1,128]{1,0:T(1,128)} %bitcast.8, f32[1,128]{1,0:T(1,128)} %bitcast.9, ...), custom_call_target="tpu_custom_call" | custom-call | tf_op jit(solution)/shard_map/pallas_call | solution.py:497
  14.3 0.6 %copy.13 = bf16[8,32,128]{2,1,0:T(8,128)(2,1)} copy(bf16[8,32,128]{2,1,0:T(8,128)(2,1)S(1)} %shard_map.109) | data formatting | bytes 131072

commit v7 on v6

--- a/solution.py
+++ b/solution.py
@@ -507,7 +507,7 @@
             pltpu.VMEM((half, tile, channels), bf16),
             pltpu.VMEM((half, tile, channels), bf16),
             pltpu.VMEM((4 * flat, channels), f32),
-            pltpu.VMEM((2 * half * flat, channels), f32),
+            pltpu.VMEM((2 * half * flat + tile_cols, channels), f32),
             pltpu.VMEM((2 * half * tile, channels), f32),
             pltpu.VMEM((flat, channels), f32),
             pltpu.VMEM((flat, channels), f32),

time: 15 us -> 15 us (level)
  no operation moved by 1% of the time
where the time goes in v7:
time: 15 us; the launch traced here: 14.9 us
  Pallas kernels  14.3 us (95%)
  local copies, waits for them, and re-layouts  0.63 us (4%)
    pallas_call x1, Pallas kernels, fused(): pl.pallas_call(functools.partial(kernel, rows, tile_rows, tile_cols), out...  14.3 us
    unnamed x1, local copies, waits for them, and re-layouts  0.63 us

profile of v7, /device:TPU:1, one launch (start us, length us, event | category | flops | bytes accessed | tf_op | source)
XLA Modules:
  0.0 14.9 jit_solution(7658633871189931522)
XLA Ops:
  0.0 14.3 %shard_map.109 = bf16[8,32,128]{2,1,0:T(8,128)(2,1)S(1)} custom-call(bf16[8,32,128]{2,1,0:T(8,128)(2,1)} %pair_h.1, s32[8,32]{1,0:T(8,128)} %mask_h.1, s32[1,64]{1,0:T(1,128)} %bitcast.5, f32[1,128]{1,0:T(1,128)} %bitcast.6, f32[1,128]{1,0:T(1,128)} %bitcast.7, f32[1,128]{1,0:T(1,128)} %bitcast.8, f32[1,128]{1,0:T(1,128)} %bitcast.9, ...), custom_call_target="tpu_custom_call" | custom-call | tf_op jit(solution)/shard_map/pallas_call | solution.py:497
  14.3 0.6 %copy.13 = bf16[8,32,128]{2,1,0:T(8,128)(2,1)} copy(bf16[8,32,128]{2,1,0:T(8,128)(2,1)S(1)} %shard_map.109) | data formatting | bytes 131072
